TPU v7x, 32 devices: a whole 2x2x4 slice. The times are simulated.
32 devices in a mesh: groups: 2 (over y), seq: 4 (over z), col: 4 (over x, core).
Axes of the slice: x: 2, y: 2, z: 4, core: 2. Of those that a mesh axis runs over, the one named last changes fastest.
Arguments:
- embeddings: bfloat16 [8192, 1280], P(('groups', 'seq'), 'col'), parts along dimension 0, may hold values from -12 to 12
- residues: int32 [8192, 1024], P(('groups', 'seq'), 'col'), parts along dimension 0, may hold values from 0 to 20
Outputs:
- sequence_weight_vector: float32 [8192], P(('groups', 'seq')), parts along dimension 0
- profile: float32 [21, 2048], P(None, ('groups', 'col')), parts along dimension 1
There are 2 independent parts, one for each index of `groups`. A program takes and returns all parts, laid end to end along the dimension named above; each array names one. Nothing has to cross between parts.
All inputs are finite; a program needn't handle non-finite values.
Results may differ from a plain program's by a relative error of at most 0.0003.
Values may be sent and summed in bfloat16 or wider, within the bound.
A program may use at most 64 MiB of HBM per device.

v0:
```python
import jax
import jax.numpy as jnp
from jax import lax
from jax.sharding import PartitionSpec as P

SYMBOLS = 21


similarity_limit = 0.5
sigmoid_sharpness_scale = 0.05


def passed_along(x, axis, by):
    size = lax.axis_size(axis)
    return lax.ppermute(x, axis, [(i, (i + by) % size) for i in range(size)])


def soft_counts(left_rows, partner, feature_length):
    pairwise_agreement = jnp.einsum(
        "id,jd->ij", left_rows, partner, preferred_element_type=jnp.float32
    )
    return jax.nn.sigmoid(
        (pairwise_agreement / feature_length - similarity_limit) / sigmoid_sharpness_scale
    )


def body(embeddings, residues):
    own_block = lax.all_gather(embeddings, "col", axis=1, tiled=True)
    feature_length = own_block.shape[1]
    row_count = own_block.shape[0]
    quarter = row_count // lax.axis_size("col")
    row_start = lax.axis_index("col") * quarter
    own_rows = lax.dynamic_slice_in_dim(own_block, row_start, quarter, 0)
    block_count = lax.axis_size("seq")
    round_count = min(4, (block_count - 1) // 2)
    stride = max(1, block_count // 8)
    nearby_counts_summed = jnp.sum(soft_counts(own_block, own_rows, feature_length), axis=1)
    for round_index in range(round_count):
        distance = 1 + round_index * stride
        for offset in (distance, -distance):
            partner = passed_along(own_rows, "seq", offset)
            nearby_counts_summed = nearby_counts_summed + jnp.sum(
                soft_counts(own_block, partner, feature_length), axis=1
            )
    own_part = lax.dynamic_slice_in_dim(nearby_counts_summed, row_start, quarter, 0)
    nearby_counts_summed = lax.dynamic_update_slice_in_dim(
        nearby_counts_summed, own_part, row_start, 0
    )
    counts = lax.psum(nearby_counts_summed, "col")
    weights = 1.0 / counts
    incomplete_frequency_table = jnp.stack(
        [
            jnp.sum(jnp.where(residues == symbol, weights[:, None], 0.0), axis=0)
            for symbol in range(SYMBOLS)
        ]
    )
    local_total = jnp.sum(weights)
    summed, weight_sum = lax.psum((incomplete_frequency_table, local_total), "seq")
    seq_count = row_count * block_count
    return (weights * (seq_count / weight_sum), summed / weight_sum)


def solution(mesh):
    return jax.shard_map(
        body,
        mesh=mesh,
        in_specs=(P(("groups", "seq"), "col"), P(("groups", "seq"), "col")),
        out_specs=(P(("groups", "seq")), P(None, ("groups", "col"))),
        check_vma=False,
    )
```

profile of v0, /device:TPU:0, one launch (start us, length us, event | category | flops | bytes accessed | tf_op | source)
XLA Modules:
  0.0 110.0 jit_solution(6116529368563728511)
XLA Ops:
  7.2 0.0 all-gather.2.cloned.1.call-start
  7.2 0.7 all-gather.2.cloned.1.call-update
  7.9 29.9 %all-gather.2.cloned.1.call-done = bf16[1024,1280]{0,1:T(8,128)(2,1)} async-done(((bf16[1024,320]{0,1:T(8,128)(2,1)}), bf16[1024,1280]{0,1:T(8,128)(2,1)}) %all-gather.2.cloned.1.call-update) | async-done | bytes 2621456 | tf_op jit(solution)/shard_map/all_gather | solution.py:28
  37.8 1.1 %constant_dynamic-slice_fusion = bf16[256,1280]{0,1:T(8,128)(2,1)S(1)} fusion(bf16[1024,1280]{0,1:T(8,128)(2,1)} %all-gather.2.cloned.1.call-done, s32[]{:T(128)S(6)} %select_n.69), kind=kLoop, calls=%fused_computation.50 | loop fusion | bytes 1310724 | tf_op jit(solution)/shard_map/dynamic_slice | solution.py:33
  39.0 0.0 copy-start.1
  39.0 1.5 %collective-permute-start = (bf16[256,1280]{0,1:T(8,128)(2,1)S(1)}, bf16[256,1280]{0,1:T(8,128)(2,1)S(1)}, u32[]{:S(2)}, u32[]{:S(2)}) collective-permute-start(bf16[256,1280]{0,1:T(8,128)(2,1)S(1)} %constant_dynamic-slice_fusion), channel_id=1, source_target_pairs={{0,4},{4,8},{8,12},{12,0},{1,5},{5,9},{9,13},{13,1},{2,6},{6,10},{... | collective-permute-start | bytes 1966088 | tf_op jit(solution)/shard_map/ppermute | solution.py:15
  40.5 2.3 %collective-permute-start.1 = (bf16[256,1280]{0,1:T(8,128)(2,1)S(1)}, bf16[256,1280]{0,1:T(8,128)(2,1)S(1)}, u32[]{:S(2)}, u32[]{:S(2)}) collective-permute-start(bf16[256,1280]{0,1:T(8,128)(2,1)S(1)} %constant_dynamic-slice_fusion), channel_id=1, source_target_pairs={{0,12},{4,0},{8,4},{12,8},{1,13},{5,1},{9,5},{13,9},{2,14},{6,2},{... | collective-permute-start | bytes 1966088 | tf_op jit(solution)/shard_map/ppermute | solution.py:15
  42.9 2.8 %fusion.18 = f32[1024]{0:T(1024)S(1)} fusion(bf16[256,1280]{0,1:T(8,128)(2,1)S(1)} %constant_dynamic-slice_fusion, bf16[1024,1280]{0,1:T(8,128)(2,1)} %all-gather.2.cloned.1.call-done), kind=kOutput, calls=%fused_computation.21 | convolution fusion | flops 672922624 | bytes 3280896 | tf_op jit(solution)/shard_map/id,jd->ij/dot_general | solution.py:19
  45.6 12.8 %collective-permute-done = bf16[256,1280]{0,1:T(8,128)(2,1)S(1)} collective-permute-done((bf16[256,1280]{0,1:T(8,128)(2,1)S(1)}, bf16[256,1280]{0,1:T(8,128)(2,1)S(1)}, u32[]{:S(2)}, u32[]{:S(2)}) %collective-permute-start) | collective-permute-done | bytes 655392 | tf_op jit(solution)/shard_map/ppermute | solution.py:15
  58.4 0.0 copy-done.1
  58.5 1.0 fusion.19
  59.5 0.0 copy-start
  59.5 11.7 %collective-permute-done.1 = bf16[256,1280]{0,1:T(8,128)(2,1)S(1)} collective-permute-done((bf16[256,1280]{0,1:T(8,128)(2,1)S(1)}, bf16[256,1280]{0,1:T(8,128)(2,1)S(1)}, u32[]{:S(2)}, u32[]{:S(2)}) %collective-permute-start.1) | collective-permute-done | bytes 655392 | tf_op jit(solution)/shard_map/ppermute | solution.py:15
  71.2 1.0 fusion.20
  72.2 0.2 dynamic-slice_dynamic-update-slice_fusion
  72.4 5.9 %psum.21 = f32[1024]{0:T(1024)S(1)} all-reduce(f32[1024]{0:T(1024)S(1)} %dynamic-slice_dynamic-update-slice_fusion), channel_id=1, replica_groups=mesh['groups'=2,'seq'=4,'col'=4] {'col'}, use_global_device_ids=true, to_apply=%region_3.0 | all-reduce | flops 1024 | bytes 8192 | tf_op jit(solution)/shard_map/psum | solution.py:49
  78.3 0.6 broadcast_divide_fusion.1
  78.9 0.0 copy-done
  78.9 2.8 %select_reduce_fusion = (f32[256]{0:T(256)S(1)}, f32[256]{0:T(256)S(1)}, f32[256]{0:T(256)S(1)}, f32[256]{0:T(256)S(1)}, f32[256]{0:T(256)S(1)}, /*index=5*/f32[...) fusion(s32[1024,256]{1,0:T(8,128)S(1)} %copy-done, ...), kind=kLoop, calls=%fused_computation.24 | loop fusion | flops 16509696 | bytes 1074176 | tf_op jit(solution)/shard_map/reduce_sum | solution.py:53
  81.7 0.1 stack.87
  81.8 18.9 %all-reduce = (f32[]{:T(128)}, f32[21,256]{1,0:T(8,128)S(1)}) all-reduce(f32[]{:T(128)} %get-tuple-element.26, f32[21,256]{1,0:T(8,128)S(1)} %stack.87), channel_id=1, replica_groups=mesh['groups'=2,'seq'=4,'col'=4] {'seq'}, use_global_device_ids=true, to_apply=%region_5.6 | all-reduce | flops 5377 | bytes 43016 | tf_op jit(solution)/shard_map/psum | solution.py:58
  100.6 1.3 %broadcast_divide_fusion = f32[21,256]{1,0:T(8,128)} fusion(f32[21,256]{1,0:T(8,128)S(1)} %get-tuple-element.24, f32[]{:T(128)} %get-tuple-element.23), kind=kLoop, calls=%fused_computation.45 | loop fusion | flops 5376 | bytes 43012 | tf_op jit(solution)/shard_map/div | solution.py:60
  102.6 0.6 broadcast_multiply_fusion
  (1 shorter events, 0.0 us)
Async XLA Ops:
  7.2 30.7 %all-gather.2.cloned.1.call-start = ((), (), s32[]{:S(2)}) async-start(), calls=%async_computation | async-start | bytes 3276800 | tf_op jit(solution)/shard_map/all_gather | solution.py:28
  39.0 19.5 %copy-start.1 = (bf16[1024,1280]{0,1:T(8,128)(2,1)S(1)}, bf16[1024,1280]{0,1:T(8,128)(2,1)}, u32[]{:S(2)}) copy-start(bf16[1024,1280]{0,1:T(8,128)(2,1)} %all-gather.2.cloned.1.call-done) | copy-start | bytes 7864324
  39.0 19.5 %collective-permute-start = (bf16[256,1280]{0,1:T(8,128)(2,1)S(1)}, bf16[256,1280]{0,1:T(8,128)(2,1)S(1)}, u32[]{:S(2)}, u32[]{:S(2)}) collective-permute-start(bf16[256,1280]{0,1:T(8,128)(2,1)S(1)} %constant_dynamic-slice_fusion), channel_id=1, source_target_pairs={{0,4},{4,8},{8,12},{12,0},{1,5},{5,9},{9,13},{13,1},{2,6},{6,10},{... | collective-permute-start | bytes 1966088 | tf_op jit(solution)/shard_map/ppermute | solution.py:15
  40.5 30.6 %collective-permute-start.1 = (bf16[256,1280]{0,1:T(8,128)(2,1)S(1)}, bf16[256,1280]{0,1:T(8,128)(2,1)S(1)}, u32[]{:S(2)}, u32[]{:S(2)}) collective-permute-start(bf16[256,1280]{0,1:T(8,128)(2,1)S(1)} %constant_dynamic-slice_fusion), channel_id=1, source_target_pairs={{0,12},{4,0},{8,4},{12,8},{1,13},{5,1},{9,5},{13,9},{2,14},{6,2},{... | collective-permute-start | bytes 1966088 | tf_op jit(solution)/shard_map/ppermute | solution.py:15
  59.5 19.4 %copy-start = (s32[1024,256]{1,0:T(8,128)S(1)}, s32[1024,256]{1,0:T(8,128)}, u32[]{:S(2)}) copy-start(s32[1024,256]{1,0:T(8,128)} %param.3) | copy-start | bytes 3145732
Sparse Core Ops, SparseCore 0:
  9.6 28.2 all-gather.1
where the time goes:
time: 110 us
  waiting for transfers between devices  55.1 us (50%)
  blocking collectives  24.7 us (22%)
  between operations  14.8 us (13%)
  other arithmetic  5.23 us (5%)
  matrix products  4.86 us (4%)
  starting transfers between devices  3.91 us (4%)
  local copies, waits for them, and re-layouts  1.41 us (1%)
    all_gather x1, waiting for transfers between devices, body(): own_block = lax.all_gather(embeddings, 'col', axis=1, tiled=True)  29.9 us
    ppermute x2, waiting for transfers between devices, passed_along(): return lax.ppermute(x, axis, [(i, (i + by) % size) for i in range(size)])  24.5 us
    psum x1, blocking collectives, body(): lax.psum((incomplete_frequency_table, local_total), 'seq')  18.9 us
    psum x1, blocking collectives, body(): counts = lax.psum(nearby_counts_summed, 'col')  5.89 us
    dot_general x3, matrix products, soft_counts(): jnp.einsum('id,jd->ij', left_rows, partner, preferred_element_type=jnp.fl...  4.86 us
    ppermute x2, starting transfers between devices, passed_along(): return lax.ppermute(x, axis, [(i, (i + by) % size) for i in range(size)])  3.88 us
    reduce_sum x1, other arithmetic, body(): jnp.sum(jnp.where(residues == symbol, weights[:, None], 0.0), axis=0)  2.76 us
  transfers between devices with their start and end apart: 3, of which 3 were waited for; matrix products, arithmetic and copies ran while one was open for 3% of the time, Pallas kernels for 0%

commit v1 on v0

v1 whole, which is shorter than its diff:
```python
import functools
import math

import jax
import jax.numpy as jnp
from jax import lax
from jax.experimental import pallas as pl
from jax.experimental.pallas import tpu as pltpu
from jax.sharding import PartitionSpec as P

SYMBOLS = 21
TABLE_ROWS = 24
COLS = 4

similarity_limit = 0.5
sigmoid_sharpness_scale = 0.05


def round_distances(block_count):
    round_count = min(4, (block_count - 1) // 2)
    stride = max(1, block_count // 8)
    return [1 + r * stride for r in range(round_count)]


def butterfly_sum(terms):
    while len(terms) > 1:
        half = len(terms) // 2
        terms = [terms[i] + terms[i + half] for i in range(half)]
    return terms[0]


def sigmoid_of(products, feature_length):
    log2e = math.log2(math.e)
    slope = -log2e / (feature_length * sigmoid_sharpness_scale)
    shift = log2e * similarity_limit / sigmoid_sharpness_scale
    return 1.0 / (1.0 + jnp.exp2(jnp.minimum(products * slope + shift, 126.0)))


def kernel(
    n, distances, quarter,
    x_ref, res_ref, weight_ref, profile_ref,
    gathered, zone, own, partner, onehot, rows_out, rows_in, back_out, back_in, table_out, table_in,
    xs, xr, ss, sr, fs, fr, zs, zr, cs, cr, ks, kr, ps, pr,
):
    width = x_ref.shape[1]
    feature_length = width * COLS
    half = quarter // 2
    me = lax.axis_index("col")
    block = lax.axis_index("seq")
    group = lax.axis_index("groups")
    cols = [me, me + 1 - 2 * (me % 2), (me + 2) % 4, 3 - me]

    def device(o, k):
        return (group, lax.rem(block + (o % n), n), cols[k])

    peers = {(0, k) for k in range(1, COLS)}
    peers |= {(s * d % n, k) for d in distances for s in (1, -1) for k in range(COLS)}
    peers |= {(o, 0) for o in range(1, n)}
    peers = sorted(peers)

    barrier = pltpu.get_barrier_semaphore()
    for o, k in peers:
        pl.semaphore_signal(
            barrier, inc=1, device_id=device(o, k), device_id_type=pl.DeviceIdType.MESH
        )
    for r in range(COLS):
        start = pl.multiple_of(cols[r] * quarter, quarter)
        rows = x_ref[pl.ds(start, quarter), :]
        gathered[0, r, 0:quarter, :] = rows[:, 0:128]
        gathered[0, r, quarter : 2 * quarter, :] = rows[:, 128:256]
        gathered[0, r, 2 * quarter : 2 * quarter + half, :] = jnp.concatenate(
            [rows[:half, 256:320], rows[half:, 256:320]], axis=1
        )
    pl.semaphore_wait(barrier, len(peers))

    started = []

    def send(src, dst, send_sem, recv_sem, o, k):
        copy = pltpu.make_async_remote_copy(
            src_ref=src, dst_ref=dst, send_sem=send_sem, recv_sem=recv_sem,
            device_id=device(o, k), device_id_type=pl.DeviceIdType.MESH,
        )
        copy.start()
        started.append(copy)

    def arrived(dst, recv_sem):
        pltpu.make_async_copy(dst, dst, recv_sem).wait()

    def send_on_z(slot):
        for i, d in enumerate(distances):
            send(gathered.at[slot, 0], zone.at[i, slot], zs.at[i, slot], zr.at[i, slot], d, 0)

    def pass_to_sibling(r):
        arrived(gathered.at[2, r], xr.at[r])
        send(gathered.at[2, r], gathered.at[3, r ^ 1], fs.at[r], fr.at[r ^ 1], 0, 1)

    for r in (3, 2, 0, 1):
        send(gathered.at[0, r], gathered.at[2, r ^ 2], xs.at[r], xr.at[r ^ 2], 0, 2)
    send_on_z(0)
    for r in (1, 0, 3, 2):
        send(gathered.at[0, r], gathered.at[1, r ^ 1], ss.at[r], sr.at[r ^ 1], 0, 1)
    arrived(gathered.at[1, 0], sr.at[0])
    send_on_z(1)

    def spread(r):
        start = pl.multiple_of(cols[r] * quarter, quarter)
        codes = res_ref[pl.ds(start, quarter), :]
        for symbol in range(SYMBOLS):
            onehot[symbol, r * quarter : (r + 1) * quarter, :] = jnp.where(
                codes == symbol, 1.0, 0.0
            ).astype(jnp.bfloat16)

    def assemble(parts, target, first):
        for slot in range(COLS):
            part = parts(slot)
            target[first : first + quarter, slot * 256 : slot * 256 + 128] = part[0:quarter, :]
            target[first : first + quarter, slot * 256 + 128 : slot * 256 + 256] = part[
                quarter : 2 * quarter, :
            ]
        for pair in range(COLS // 2):
            one = parts(2 * pair)[2 * quarter : 2 * quarter + half, :]
            two = parts(2 * pair + 1)[2 * quarter : 2 * quarter + half, :]
            at = COLS * 256 + pair * 128
            target[first : first + half, at : at + 128] = jnp.concatenate(
                [one[:, :64], two[:, :64]], axis=1
            )
            target[first + half : first + quarter, at : at + 128] = jnp.concatenate(
                [one[:, 64:], two[:, 64:]], axis=1
            )

    def agreement(left, r):
        products = lax.dot_general(
            left, own[r * quarter : (r + 1) * quarter, :],
            (((1,), (1,)), ((), ())), preferred_element_type=jnp.float32,
        )
        return sigmoid_of(products, feature_length)

    spread(0)
    pass_to_sibling(1)
    pass_to_sibling(0)
    send_on_z(2)
    arrived(gathered.at[3, 0], fr.at[0])
    send_on_z(3)
    sums = []
    for r in range(COLS):
        if r > 0:
            spread(r)
        if r > 1:
            pass_to_sibling(r)
        if r == 1 or r == 3:
            for q in (r - 1, r):
                if q > 0:
                    arrived(gathered.at[1, q], sr.at[q])
                    arrived(gathered.at[3, q], fr.at[q])
                assemble(lambda slot: gathered[slot, q], own, q * quarter)
                sums.append(
                    jnp.sum(agreement(own[0:quarter, :], q), axis=0, keepdims=True)
                )

    for i, d in enumerate(distances):
        for slot in range(COLS):
            arrived(zone.at[i, slot], zr.at[i, slot])
        assemble(lambda slot: zone[i, slot], partner, 0)
        across = jnp.zeros((quarter, 128), jnp.float32)
        for r in range(COLS):
            values = agreement(partner[...], r)
            sums[r] = sums[r] + jnp.sum(values, axis=0, keepdims=True)
            for lane in range(0, quarter, 128):
                across = across + values[:, lane : lane + 128]
        back = jnp.sum(across.T, axis=0, keepdims=True)
        back_out[i] = jnp.broadcast_to(back, (8, quarter))
        for k in range(COLS):
            send(back_out.at[i], back_in.at[i, k], ks.at[i, k], kr.at[i, k], -d, k)
    for r in range(COLS):
        rows_out[r : r + 1, :] = sums[r]
        rows_out[r + COLS : r + COLS + 1, :] = sums[r]
    for k in range(1, COLS):
        send(rows_out, rows_in.at[k], cs.at[k], cr.at[k], 0, k)
    for k in range(1, COLS):
        arrived(rows_in.at[k], cr.at[k])
    for i in range(len(distances)):
        for k in range(COLS):
            arrived(back_in.at[i, k], kr.at[i, k])

    weights = []
    for r in range(COLS):
        terms = [sums[r]] + [rows_in[k, r ^ k : (r ^ k) + 1, :] for k in range(1, COLS)]
        counts = (terms[0] + terms[1]) + (terms[2] + terms[3])
        for i in range(len(distances)):
            counts = counts + back_in[i, r, 0:1, :]
        weights.append(1.0 / counts)
    local_total = jnp.sum(
        (weights[0] + weights[1]) + (weights[2] + weights[3]), axis=1, keepdims=True
    )

    whole = jnp.concatenate(weights, axis=1)
    high = whole.astype(jnp.bfloat16).astype(jnp.float32)
    rest = whole - high
    middle = rest.astype(jnp.bfloat16).astype(jnp.float32)
    low = rest - middle
    row = lax.broadcasted_iota(jnp.int32, (16, whole.shape[1]), 0)
    split = jnp.where(
        row == 0, high, jnp.where(row == 1, middle, jnp.where(row == 2, low, 0.0))
    ).astype(jnp.bfloat16)
    for symbol in range(SYMBOLS):
        part = jnp.dot(split, onehot[symbol], preferred_element_type=jnp.float32)
        table_out[symbol : symbol + 1, :] = jnp.sum(part, axis=0, keepdims=True)
    table_out[SYMBOLS:TABLE_ROWS, :] = jnp.broadcast_to(
        local_total, (TABLE_ROWS - SYMBOLS, table_out.shape[1])
    )
    for o in range(1, n):
        send(table_out, table_in.at[o], ps.at[o], pr.at[o], o, 0)
    for o in range(1, n):
        arrived(table_in.at[o], pr.at[o])
    table = butterfly_sum([table_out[...]] + [table_in[o] for o in range(1, n)])
    weight_sum = table[SYMBOLS : SYMBOLS + 1, :]
    profile_ref[...] = table[:SYMBOLS, :] / weight_sum
    scale = (n * COLS * quarter) / weight_sum
    for r in range(COLS):
        scaled = weights[r] * scale
        for piece in range(quarter // 128):
            weight_ref[pl.ds(cols[r] * (quarter // 128) + piece, 1), :] = scaled[
                :, piece * 128 : piece * 128 + 128
            ]
    for copy in started:
        copy.wait_send()


def body(n, embeddings, residues):
    rows, width = embeddings.shape
    columns = residues.shape[1]
    quarter = rows // COLS
    distances = round_distances(n)
    nd = len(distances)
    packed = quarter * width // 128
    dma = pltpu.SemaphoreType.DMA
    weights, profile = pl.pallas_call(
        functools.partial(kernel, n, distances, quarter),
        out_shape=(
            jax.ShapeDtypeStruct((rows // 128, 128), jnp.float32),
            jax.ShapeDtypeStruct((SYMBOLS, columns), jnp.float32),
        ),
        in_specs=[pl.BlockSpec(memory_space=pltpu.VMEM)] * 2,
        out_specs=[pl.BlockSpec(memory_space=pltpu.VMEM)] * 2,
        scratch_shapes=[
            pltpu.VMEM((COLS, COLS, packed, 128), jnp.bfloat16),
            pltpu.VMEM((nd, COLS, packed, 128), jnp.bfloat16),
            pltpu.VMEM((rows, width * COLS), jnp.bfloat16),
            pltpu.VMEM((quarter, width * COLS), jnp.bfloat16),
            pltpu.VMEM((SYMBOLS, rows, columns), jnp.bfloat16),
            pltpu.VMEM((8, quarter), jnp.float32),
            pltpu.VMEM((COLS, 8, quarter), jnp.float32),
            pltpu.VMEM((nd, 8, quarter), jnp.float32),
            pltpu.VMEM((nd, COLS, 8, quarter), jnp.float32),
            pltpu.VMEM((TABLE_ROWS, columns), jnp.float32),
            pltpu.VMEM((n, TABLE_ROWS, columns), jnp.float32),
            dma((COLS,)), dma((COLS,)), dma((COLS,)), dma((COLS,)), dma((COLS,)), dma((COLS,)),
            dma((nd, COLS)), dma((nd, COLS)), dma((COLS,)), dma((COLS,)),
            dma((nd, COLS)), dma((nd, COLS)), dma((n,)), dma((n,)),
        ],
        compiler_params=pltpu.CompilerParams(
            collective_id=0, has_side_effects=True, vmem_limit_bytes=48 * 1024 * 1024
        ),
    )(embeddings, residues)
    return weights.reshape(rows), profile


def solution(mesh):
    return jax.shard_map(
        functools.partial(body, mesh.shape["seq"]),
        mesh=mesh,
        in_specs=(P(("groups", "seq"), "col"), P(("groups", "seq"), "col")),
        out_specs=(P(("groups", "seq")), P(None, ("groups", "col"))),
        check_vma=False,
    )
```

time: 110 us -> 38.8 us (0.35)
  waiting for transfers between devices: 55.1 us -> 0 us
  Pallas kernels: 0 us -> 35.3 us
  blocking collectives: 24.7 us -> 0 us
  between operations: 14.8 us -> 0.66 us
  other arithmetic: 5.23 us -> 0 us
  matrix products: 4.86 us -> 0 us
  starting transfers between devices: 3.91 us -> 0 us
  local copies, waits for them, and re-layouts: 1.41 us -> 2.73 us
    pallas_call x0 -> x1, Pallas kernels: none -> 35.3 us  [body(): pl.pallas_call(functools.partial(kernel, n, distances, quarter), out_shap...]
    all_gather x1 -> x0, waiting for transfers between devices: 29.9 us -> none  [body(): own_block = lax.all_gather(embeddings, 'col', axis=1, tiled=True)]
    psum x2 -> x0, blocking collectives: 24.7 us -> none  [the longest x1 18.9 us: body(): lax.psum((incomplete_frequency_table, local_total), 'seq')]
    ppermute x2 -> x0, waiting for transfers between devices: 24.5 us -> none  [passed_along(): return lax.ppermute(x, axis, [(i, (i + by) % size) for i in range(size)])]
    dot_general x3 -> x0, matrix products: 4.86 us -> none  [soft_counts(): jnp.einsum('id,jd->ij', left_rows, partner, preferred_element_type=jnp.fl...]
    ppermute x2 -> x0, starting transfers between devices: 3.88 us -> none  [passed_along(): return lax.ppermute(x, axis, [(i, (i + by) % size) for i in range(size)])]
    reduce_sum x1 -> x0, other arithmetic: 2.76 us -> none  [body(): jnp.sum(jnp.where(residues == symbol, weights[:, None], 0.0), axis=0)]
    unnamed x4 -> x5, local copies, waits for them, and re-layouts: 0.01 us -> 2.73 us
  transfers between devices with their start and end apart: 3 -> 0, of which waited for: 3 -> 0; matrix products, arithmetic and copies ran while one was open for 3% -> 0% of each run, Pallas kernels for 0% -> 0%
where the time goes in v1:
time: 38.8 us; the launch traced here: 38.7 us
  Pallas kernels  35.3 us (91%)
  local copies, waits for them, and re-layouts  2.73 us (7%)
  between operations  0.66 us (2%)
    pallas_call x1, Pallas kernels, body(): pl.pallas_call(functools.partial(kernel, n, distances, quarter), out_shap...  35.3 us
    unnamed x5, local copies, waits for them, and re-layouts  2.73 us

profile of v1, /device:TPU:0, one launch (start us, length us, event | category | flops | bytes accessed | tf_op | source)
XLA Modules:
  0.0 38.7 jit_solution(13072051465034471605)
XLA Ops:
  0.6 0.0 copy-start
  0.6 1.5 %copy.4.x_ref = bf16[1024,320]{1,0:T(8,128)(2,1)S(1)} copy(bf16[1024,320]{0,1:T(8,128)(2,1)} %param.2) | data formatting | bytes 1310720 | tf_op args[0]
  2.2 0.0 copy-done
  2.2 35.3 %shard_map.41 = (f32[8,128]{1,0:T(8,128)S(1)}, f32[21,256]{1,0:T(8,128)S(1)}) custom-call(bf16[1024,320]{1,0:T(8,128)(2,1)S(1)} %copy.4.x_ref, s32[1024,256]{1,0:T(8,128)S(1)} %copy-done), custom_call_target="tpu_custom_call" | custom-call | tf_op jit(solution)/shard_map/pallas_call | solution.py:237
  37.5 0.6 %copy.7 = f32[1024]{0:T(1024)} copy(f32[1024]{0:T(1024)S(1)} %bitcast.1) | data formatting | bytes 8192
  38.1 0.6 %copy.8 = f32[21,256]{1,0:T(8,128)} copy(f32[21,256]{1,0:T(8,128)S(1)} %get-tuple-element.9) | data formatting | bytes 43008
Async XLA Ops:
  0.6 1.5 %copy-start = (s32[1024,256]{1,0:T(8,128)S(1)}, s32[1024,256]{1,0:T(8,128)}, u32[]{:S(2)}) copy-start(s32[1024,256]{1,0:T(8,128)} %res_ref.1) | copy-start | bytes 3145732

commit v2 on v1

--- a/solution.py
+++ b/solution.py
@@ -39,12 +39,11 @@
 def kernel(
     n, distances, quarter,
     x_ref, res_ref, weight_ref, profile_ref,
-    gathered, zone, own, partner, onehot, rows_out, rows_in, back_out, back_in, table_out, table_in,
-    xs, xr, ss, sr, fs, fr, zs, zr, cs, cr, ks, kr, ps, pr,
+    gathered, zone, left, residues, onehot, rows_out, rows_in, back_out, back_in, table_out, table_in,
+    ls, rs, xs, xr, ss, sr, fs, fr, zs, zr, cs, cr, ks, kr, ps, pr,
 ):
-    width = x_ref.shape[1]
+    width = x_ref.shape[0]
     feature_length = width * COLS
-    half = quarter // 2
     me = lax.axis_index("col")
     block = lax.axis_index("seq")
     group = lax.axis_index("groups")
@@ -52,6 +51,9 @@
 
     def device(o, k):
         return (group, lax.rem(block + (o % n), n), cols[k])
+
+    def piece(slot, r):
+        return gathered.at[r, pl.ds(slot * width, width), :]
 
     peers = {(0, k) for k in range(1, COLS)}
     peers |= {(s * d % n, k) for d in distances for s in (1, -1) for k in range(COLS)}
@@ -63,14 +65,18 @@
         pl.semaphore_signal(
             barrier, inc=1, device_id=device(o, k), device_id_type=pl.DeviceIdType.MESH
         )
-    for r in range(COLS):
+    loads = []
+    for r in (3, 2, 0, 1):
         start = pl.multiple_of(cols[r] * quarter, quarter)
-        rows = x_ref[pl.ds(start, quarter), :]
-        gathered[0, r, 0:quarter, :] = rows[:, 0:128]
-        gathered[0, r, quarter : 2 * quarter, :] = rows[:, 128:256]
-        gathered[0, r, 2 * quarter : 2 * quarter + half, :] = jnp.concatenate(
-            [rows[:half, 256:320], rows[half:, 256:320]], axis=1
+        loads.append(
+            pltpu.make_async_copy(x_ref.at[:, pl.ds(start, quarter)], piece(0, r), ls.at[r])
         )
+    fetch_residues = pltpu.make_async_copy(res_ref, residues, rs)
+    for load in loads:
+        load.start()
+    fetch_residues.start()
+    for load in loads:
+        load.wait()
     pl.semaphore_wait(barrier, len(peers))
 
     started = []
@@ -88,58 +94,41 @@
 
     def send_on_z(slot):
         for i, d in enumerate(distances):
-            send(gathered.at[slot, 0], zone.at[i, slot], zs.at[i, slot], zr.at[i, slot], d, 0)
+            send(
+                piece(slot, 0), zone.at[i, pl.ds(slot * width, width), :],
+                zs.at[i, slot], zr.at[i, slot], d, 0,
+            )
 
     def pass_to_sibling(r):
-        arrived(gathered.at[2, r], xr.at[r])
-        send(gathered.at[2, r], gathered.at[3, r ^ 1], fs.at[r], fr.at[r ^ 1], 0, 1)
+        arrived(piece(2, r), xr.at[r])
+        send(piece(2, r), piece(3, r ^ 1), fs.at[r], fr.at[r ^ 1], 0, 1)
 
     for r in (3, 2, 0, 1):
-        send(gathered.at[0, r], gathered.at[2, r ^ 2], xs.at[r], xr.at[r ^ 2], 0, 2)
+        send(piece(0, r), piece(2, r ^ 2), xs.at[r], xr.at[r ^ 2], 0, 2)
     send_on_z(0)
     for r in (1, 0, 3, 2):
-        send(gathered.at[0, r], gathered.at[1, r ^ 1], ss.at[r], sr.at[r ^ 1], 0, 1)
-    arrived(gathered.at[1, 0], sr.at[0])
+        send(piece(0, r), piece(1, r ^ 1), ss.at[r], sr.at[r ^ 1], 0, 1)
+    arrived(piece(1, 0), sr.at[0])
     send_on_z(1)
+    fetch_residues.wait()
 
     def spread(r):
         start = pl.multiple_of(cols[r] * quarter, quarter)
-        codes = res_ref[pl.ds(start, quarter), :]
+        codes = residues[pl.ds(start, quarter), :]
         for symbol in range(SYMBOLS):
             onehot[symbol, r * quarter : (r + 1) * quarter, :] = jnp.where(
                 codes == symbol, 1.0, 0.0
             ).astype(jnp.bfloat16)
 
-    def assemble(parts, target, first):
-        for slot in range(COLS):
-            part = parts(slot)
-            target[first : first + quarter, slot * 256 : slot * 256 + 128] = part[0:quarter, :]
-            target[first : first + quarter, slot * 256 + 128 : slot * 256 + 256] = part[
-                quarter : 2 * quarter, :
-            ]
-        for pair in range(COLS // 2):
-            one = parts(2 * pair)[2 * quarter : 2 * quarter + half, :]
-            two = parts(2 * pair + 1)[2 * quarter : 2 * quarter + half, :]
-            at = COLS * 256 + pair * 128
-            target[first : first + half, at : at + 128] = jnp.concatenate(
-                [one[:, :64], two[:, :64]], axis=1
-            )
-            target[first + half : first + quarter, at : at + 128] = jnp.concatenate(
-                [one[:, 64:], two[:, 64:]], axis=1
-            )
-
-    def agreement(left, r):
-        products = lax.dot_general(
-            left, own[r * quarter : (r + 1) * quarter, :],
-            (((1,), (1,)), ((), ())), preferred_element_type=jnp.float32,
-        )
+    def agreement(r):
+        products = jnp.dot(left[...], gathered[r], preferred_element_type=jnp.float32)
         return sigmoid_of(products, feature_length)
 
     spread(0)
     pass_to_sibling(1)
     pass_to_sibling(0)
     send_on_z(2)
-    arrived(gathered.at[3, 0], fr.at[0])
+    arrived(piece(3, 0), fr.at[0])
     send_on_z(3)
     sums = []
     for r in range(COLS):
@@ -150,20 +139,19 @@
         if r == 1 or r == 3:
             for q in (r - 1, r):
                 if q > 0:
-                    arrived(gathered.at[1, q], sr.at[q])
-                    arrived(gathered.at[3, q], fr.at[q])
-                assemble(lambda slot: gathered[slot, q], own, q * quarter)
-                sums.append(
-                    jnp.sum(agreement(own[0:quarter, :], q), axis=0, keepdims=True)
-                )
+                    arrived(piece(1, q), sr.at[q])
+                    arrived(piece(3, q), fr.at[q])
+                else:
+                    left[...] = gathered[0].T
+                sums.append(jnp.sum(agreement(q), axis=0, keepdims=True))
 
     for i, d in enumerate(distances):
         for slot in range(COLS):
-            arrived(zone.at[i, slot], zr.at[i, slot])
-        assemble(lambda slot: zone[i, slot], partner, 0)
+            arrived(zone.at[i, pl.ds(slot * width, width), :], zr.at[i, slot])
+        left[...] = zone[i].T
         across = jnp.zeros((quarter, 128), jnp.float32)
         for r in range(COLS):
-            values = agreement(partner[...], r)
+            values = agreement(r)
             sums[r] = sums[r] + jnp.sum(values, axis=0, keepdims=True)
             for lane in range(0, quarter, 128):
                 across = across + values[:, lane : lane + 128]
@@ -218,9 +206,9 @@
     scale = (n * COLS * quarter) / weight_sum
     for r in range(COLS):
         scaled = weights[r] * scale
-        for piece in range(quarter // 128):
-            weight_ref[pl.ds(cols[r] * (quarter // 128) + piece, 1), :] = scaled[
-                :, piece * 128 : piece * 128 + 128
+        for part in range(quarter // 128):
+            weight_ref[pl.ds(cols[r] * (quarter // 128) + part, 1), :] = scaled[
+                :, part * 128 : part * 128 + 128
             ]
     for copy in started:
         copy.wait_send()
@@ -232,7 +220,6 @@
     quarter = rows // COLS
     distances = round_distances(n)
     nd = len(distances)
-    packed = quarter * width // 128
     dma = pltpu.SemaphoreType.DMA
     weights, profile = pl.pallas_call(
         functools.partial(kernel, n, distances, quarter),
@@ -240,13 +227,13 @@
             jax.ShapeDtypeStruct((rows // 128, 128), jnp.float32),
             jax.ShapeDtypeStruct((SYMBOLS, columns), jnp.float32),
         ),
-        in_specs=[pl.BlockSpec(memory_space=pltpu.VMEM)] * 2,
+        in_specs=[pl.BlockSpec(memory_space=pltpu.HBM)] * 2,
         out_specs=[pl.BlockSpec(memory_space=pltpu.VMEM)] * 2,
         scratch_shapes=[
-            pltpu.VMEM((COLS, COLS, packed, 128), jnp.bfloat16),
-            pltpu.VMEM((nd, COLS, packed, 128), jnp.bfloat16),
-            pltpu.VMEM((rows, width * COLS), jnp.bfloat16),
+            pltpu.VMEM((COLS, width * COLS, quarter), jnp.bfloat16),
+            pltpu.VMEM((nd, width * COLS, quarter), jnp.bfloat16),
             pltpu.VMEM((quarter, width * COLS), jnp.bfloat16),
+            pltpu.VMEM((rows, columns), jnp.int32),
             pltpu.VMEM((SYMBOLS, rows, columns), jnp.bfloat16),
             pltpu.VMEM((8, quarter), jnp.float32),
             pltpu.VMEM((COLS, 8, quarter), jnp.float32),
@@ -254,6 +241,7 @@
             pltpu.VMEM((nd, COLS, 8, quarter), jnp.float32),
             pltpu.VMEM((TABLE_ROWS, columns), jnp.float32),
             pltpu.VMEM((n, TABLE_ROWS, columns), jnp.float32),
+            dma((COLS,)), dma,
             dma((COLS,)), dma((COLS,)), dma((COLS,)), dma((COLS,)), dma((COLS,)), dma((COLS,)),
             dma((nd, COLS)), dma((nd, COLS)), dma((COLS,)), dma((COLS,)),
             dma((nd, COLS)), dma((nd, COLS)), dma((n,)), dma((n,)),
@@ -261,7 +249,7 @@
         compiler_params=pltpu.CompilerParams(
             collective_id=0, has_side_effects=True, vmem_limit_bytes=48 * 1024 * 1024
         ),
-    )(embeddings, residues)
+    )(embeddings.T, residues)
     return weights.reshape(rows), profile
 
 

time: 38.8 us -> 39.5 us (1.018)
  local copies, waits for them, and re-layouts: 2.73 us -> 3.51 us
    unnamed x5 -> x6, local copies, waits for them, and re-layouts: 2.73 us -> 3.51 us
where the time goes in v2:
time: 39.5 us; the launch traced here: 39.3 us
  Pallas kernels  35.2 us (89%)
  local copies, waits for them, and re-layouts  3.51 us (9%)
  between operations  0.65 us (2%)
    pallas_call x1, Pallas kernels, body(): pl.pallas_call(functools.partial(kernel, n, distances, quarter), out_shap...  35.2 us
    unnamed x6, local copies, waits for them, and re-layouts  3.51 us

profile of v2, /device:TPU:0, one launch (start us, length us, event | category | flops | bytes accessed | tf_op | source)
XLA Modules:
  0.0 39.3 jit_solution(15957789965155128769)
XLA Ops:
  0.6 0.0 copy-start
  0.6 1.2 %copy-done = s32[1024,256]{1,0:T(8,128)S(1)} copy-done((s32[1024,256]{1,0:T(8,128)S(1)}, s32[1024,256]{1,0:T(8,128)}, u32[]{:S(2)}) %copy-start) | copy-done | bytes 1048600
  1.9 0.0 copy-start.1
  1.9 1.1 %copy-done.1 = bf16[1024,320]{0,1:T(8,128)(2,1)S(1)} copy-done((bf16[1024,320]{0,1:T(8,128)(2,1)S(1)}, bf16[1024,320]{0,1:T(8,128)(2,1)}, u32[]{:S(2)}) %copy-start.1) | copy-done | bytes 655384
  2.9 35.2 %shard_map.41 = (f32[8,128]{1,0:T(8,128)S(1)}, f32[21,256]{1,0:T(8,128)S(1)}) custom-call(bf16[320,1024]{1,0:T(8,128)(2,1)S(1)} %bitcast.2, s32[1024,256]{1,0:T(8,128)S(1)} %copy-done), custom_call_target="tpu_custom_call" | custom-call | tf_op jit(solution)/shard_map/pallas_call | solution.py:224
  38.1 0.6 %copy.6 = f32[1024]{0:T(1024)} copy(f32[1024]{0:T(1024)S(1)} %bitcast.3) | data formatting | bytes 8192
  38.7 0.6 %copy.7 = f32[21,256]{1,0:T(8,128)} copy(f32[21,256]{1,0:T(8,128)S(1)} %get-tuple-element.9) | data formatting | bytes 43008
Async XLA Ops:
  0.6 1.2 %copy-start = (s32[1024,256]{1,0:T(8,128)S(1)}, s32[1024,256]{1,0:T(8,128)}, u32[]{:S(2)}) copy-start(s32[1024,256]{1,0:T(8,128)} %res_ref.1) | copy-start | bytes 3145732
  1.9 1.1 %copy-start.1 = (bf16[1024,320]{0,1:T(8,128)(2,1)S(1)}, bf16[1024,320]{0,1:T(8,128)(2,1)}, u32[]{:S(2)}) copy-start(bf16[1024,320]{0,1:T(8,128)(2,1)} %param.2) | copy-start | bytes 1966084

commit v3 on v2

--- a/solution.py
+++ b/solution.py
@@ -106,7 +106,7 @@
     for r in (3, 2, 0, 1):
         send(piece(0, r), piece(2, r ^ 2), xs.at[r], xr.at[r ^ 2], 0, 2)
     send_on_z(0)
-    for r in (1, 0, 3, 2):
+    for r in (1,):
         send(piece(0, r), piece(1, r ^ 1), ss.at[r], sr.at[r ^ 1], 0, 1)
     arrived(piece(1, 0), sr.at[0])
     send_on_z(1)
@@ -127,6 +127,8 @@
     spread(0)
     pass_to_sibling(1)
     pass_to_sibling(0)
+    for r in (0, 3, 2):
+        send(piece(0, r), piece(1, r ^ 1), ss.at[r], sr.at[r ^ 1], 0, 1)
     send_on_z(2)
     arrived(piece(3, 0), fr.at[0])
     send_on_z(3)
@@ -190,16 +192,22 @@
     split = jnp.where(
         row == 0, high, jnp.where(row == 1, middle, jnp.where(row == 2, low, 0.0))
     ).astype(jnp.bfloat16)
-    for symbol in range(SYMBOLS):
-        part = jnp.dot(split, onehot[symbol], preferred_element_type=jnp.float32)
-        table_out[symbol : symbol + 1, :] = jnp.sum(part, axis=0, keepdims=True)
     table_out[SYMBOLS:TABLE_ROWS, :] = jnp.broadcast_to(
         local_total, (TABLE_ROWS - SYMBOLS, table_out.shape[1])
     )
-    for o in range(1, n):
-        send(table_out, table_in.at[o], ps.at[o], pr.at[o], o, 0)
-    for o in range(1, n):
-        arrived(table_in.at[o], pr.at[o])
+    offsets = sorted(range(1, n), key=lambda o: -min(o, n - o))
+    for part in range(TABLE_ROWS // 8):
+        for symbol in range(8 * part, min(8 * part + 8, SYMBOLS)):
+            product = jnp.dot(split, onehot[symbol], preferred_element_type=jnp.float32)
+            table_out[symbol : symbol + 1, :] = jnp.sum(product, axis=0, keepdims=True)
+        for o in offsets:
+            send(
+                table_out.at[pl.ds(8 * part, 8), :], table_in.at[o, pl.ds(8 * part, 8), :],
+                ps.at[o, part], pr.at[o, part], o, 0,
+            )
+    for part in range(TABLE_ROWS // 8):
+        for o in range(1, n):
+            arrived(table_in.at[o, pl.ds(8 * part, 8), :], pr.at[o, part])
     table = butterfly_sum([table_out[...]] + [table_in[o] for o in range(1, n)])
     weight_sum = table[SYMBOLS : SYMBOLS + 1, :]
     profile_ref[...] = table[:SYMBOLS, :] / weight_sum
@@ -212,6 +220,11 @@
             ]
     for copy in started:
         copy.wait_send()
+
+
+def hand_over(weight_ref, profile_ref, weight_out, profile_out):
+    weight_out[...] = weight_ref[...]
+    profile_out[...] = profile_ref[...]
 
 
 def body(n, embeddings, residues):
@@ -244,12 +257,19 @@
             dma((COLS,)), dma,
             dma((COLS,)), dma((COLS,)), dma((COLS,)), dma((COLS,)), dma((COLS,)), dma((COLS,)),
             dma((nd, COLS)), dma((nd, COLS)), dma((COLS,)), dma((COLS,)),
-            dma((nd, COLS)), dma((nd, COLS)), dma((n,)), dma((n,)),
+            dma((nd, COLS)), dma((nd, COLS)), dma((n, TABLE_ROWS // 8)), dma((n, TABLE_ROWS // 8)),
         ],
         compiler_params=pltpu.CompilerParams(
-            collective_id=0, has_side_effects=True, vmem_limit_bytes=48 * 1024 * 1024
+            collective_id=0, has_side_effects=True, vmem_limit_bytes=62 * 1024 * 1024
         ),
     )(embeddings.T, residues)
+    weights, profile = pl.pallas_call(
+        hand_over,
+        out_shape=(
+            jax.ShapeDtypeStruct(weights.shape, jnp.float32),
+            jax.ShapeDtypeStruct(profile.shape, jnp.float32),
+        ),
+    )(weights, profile)
     return weights.reshape(rows), profile
 
 

time: 39.5 us -> 38.1 us (0.965)
  local copies, waits for them, and re-layouts: 3.51 us -> 0 us
  Pallas kernels: 35.2 us -> 37.3 us
    unnamed x6 -> x0, local copies, waits for them, and re-layouts: 3.51 us -> none
    pallas_call x0 -> x1, Pallas kernels: none -> 1.36 us  [body(): pl.pallas_call(hand_over, out_shape=(jax.ShapeDtypeStruct(weights.shape,...]
    pallas_call x1, Pallas kernels: 35.2 us -> 35.9 us  [body(): pl.pallas_call(functools.partial(kernel, n, distances, quarter), out_shap...]
where the time goes in v3:
time: 38.1 us; the launch traced here: 37.9 us
  Pallas kernels  37.3 us (98%)
  between operations  0.64 us (2%)
    pallas_call x1, Pallas kernels, body(): pl.pallas_call(functools.partial(kernel, n, distances, quarter), out_shap...  35.9 us
    pallas_call x1, Pallas kernels, body(): pl.pallas_call(hand_over, out_shape=(jax.ShapeDtypeStruct(weights.shape,...  1.36 us

profile of v3, /device:TPU:0, one launch (start us, length us, event | category | flops | bytes accessed | tf_op | source)
XLA Modules:
  0.0 37.9 jit_solution(16143039609669145928)
XLA Ops:
  0.6 35.9 %shard_map.41 = (f32[8,128]{1,0:T(8,128)}, f32[21,256]{1,0:T(8,128)}) custom-call(bf16[320,1024]{1,0:T(8,128)(2,1)} %bitcast.2, s32[1024,256]{1,0:T(8,128)} %res_ref.1), custom_call_target="tpu_custom_call" | custom-call | tf_op jit(solution)/shard_map/pallas_call | solution.py:237
  36.5 1.4 %shard_map.42 = (f32[8,128]{1,0:T(8,128)}, f32[21,256]{1,0:T(8,128)}) custom-call(f32[8,128]{1,0:T(8,128)} %get-tuple-element.6.weight_ref, f32[21,256]{1,0:T(8,128)} %get-tuple-element.7.profile_ref), custom_call_target="tpu_custom_call" | custom-call | tf_op jit(solution)/shard_map/pallas_call | solution.py:266

commit v4 on v3

--- a/solution.py
+++ b/solution.py
@@ -120,40 +120,48 @@
                 codes == symbol, 1.0, 0.0
             ).astype(jnp.bfloat16)
 
-    def agreement(r):
-        products = jnp.dot(left[...], gathered[r], preferred_element_type=jnp.float32)
+    def agreement(which, r):
+        products = jnp.dot(left[which], gathered[r], preferred_element_type=jnp.float32)
         return sigmoid_of(products, feature_length)
 
     spread(0)
     pass_to_sibling(1)
+    arrived(piece(3, 0), fr.at[0])
+    send_on_z(3)
     pass_to_sibling(0)
+    send_on_z(2)
     for r in (0, 3, 2):
         send(piece(0, r), piece(1, r ^ 1), ss.at[r], sr.at[r ^ 1], 0, 1)
-    send_on_z(2)
-    arrived(piece(3, 0), fr.at[0])
-    send_on_z(3)
     sums = []
-    for r in range(COLS):
+
+    def add_own(r):
         if r > 0:
-            spread(r)
-        if r > 1:
-            pass_to_sibling(r)
-        if r == 1 or r == 3:
-            for q in (r - 1, r):
-                if q > 0:
-                    arrived(piece(1, q), sr.at[q])
-                    arrived(piece(3, q), fr.at[q])
-                else:
-                    left[...] = gathered[0].T
-                sums.append(jnp.sum(agreement(q), axis=0, keepdims=True))
+            arrived(piece(1, r), sr.at[r])
+            arrived(piece(3, r), fr.at[r])
+        else:
+            left[0] = gathered[0].T
+        sums.append(jnp.sum(agreement(0, r), axis=0, keepdims=True))
+
+    spread(1)
+    add_own(0)
+    add_own(1)
+    spread(2)
+    pass_to_sibling(2)
+    spread(3)
+    pass_to_sibling(3)
+    add_own(2)
+    if not distances:
+        add_own(3)
 
     for i, d in enumerate(distances):
         for slot in range(COLS):
             arrived(zone.at[i, pl.ds(slot * width, width), :], zr.at[i, slot])
-        left[...] = zone[i].T
+        left[1] = zone[i].T
         across = jnp.zeros((quarter, 128), jnp.float32)
         for r in range(COLS):
-            values = agreement(r)
+            if r == len(sums):
+                add_own(r)
+            values = agreement(1, r)
             sums[r] = sums[r] + jnp.sum(values, axis=0, keepdims=True)
             for lane in range(0, quarter, 128):
                 across = across + values[:, lane : lane + 128]
@@ -245,7 +253,7 @@
         scratch_shapes=[
             pltpu.VMEM((COLS, width * COLS, quarter), jnp.bfloat16),
             pltpu.VMEM((nd, width * COLS, quarter), jnp.bfloat16),
-            pltpu.VMEM((quarter, width * COLS), jnp.bfloat16),
+            pltpu.VMEM((2, quarter, width * COLS), jnp.bfloat16),
             pltpu.VMEM((rows, columns), jnp.int32),
             pltpu.VMEM((SYMBOLS, rows, columns), jnp.bfloat16),
             pltpu.VMEM((8, quarter), jnp.float32),

time: 38.1 us -> 38.1 us (level)
  no operation moved by 1% of the time
where the time goes in v4:
time: 38.1 us; the launch traced here: 37.9 us
  Pallas kernels  37.3 us (98%)
  between operations  0.64 us (2%)
    pallas_call x1, Pallas kernels, body(): pl.pallas_call(functools.partial(kernel, n, distances, quarter), out_shap...  35.9 us
    pallas_call x1, Pallas kernels, body(): pl.pallas_call(hand_over, out_shape=(jax.ShapeDtypeStruct(weights.shape,...  1.36 us

profile of v4, /device:TPU:0, one launch (start us, length us, event | category | flops | bytes accessed | tf_op | source)
XLA Modules:
  0.0 37.9 jit_solution(3778642300453720851)
XLA Ops:
  0.6 35.9 %shard_map.41 = (f32[8,128]{1,0:T(8,128)}, f32[21,256]{1,0:T(8,128)}) custom-call(bf16[320,1024]{1,0:T(8,128)(2,1)} %bitcast.2, s32[1024,256]{1,0:T(8,128)} %res_ref.1), custom_call_target="tpu_custom_call" | custom-call | tf_op jit(solution)/shard_map/pallas_call | solution.py:245
  36.6 1.4 %shard_map.42 = (f32[8,128]{1,0:T(8,128)}, f32[21,256]{1,0:T(8,128)}) custom-call(f32[8,128]{1,0:T(8,128)} %get-tuple-element.6.weight_ref, f32[21,256]{1,0:T(8,128)} %get-tuple-element.7.profile_ref), custom_call_target="tpu_custom_call" | custom-call | tf_op jit(solution)/shard_map/pallas_call | solution.py:274
